TPU v7x, 32 devices: a whole 2x2x4 slice. The times are simulated.
32 devices in a mesh: groups: 2 (over y), dc: 4 (over z), tp: 2 (over x), sp: 2 (over core).
Axes of the slice: x: 2, y: 2, z: 4, core: 2. Of those that a mesh axis runs over, the one named last changes fastest.
Arguments:
- q_gen: bfloat16 [2048, 8192], P(('groups', 'dc', 'sp'), 'tp'), parts along dimension 0, may hold values from -32 to 32
- k_gen: bfloat16 [2048, 1024], P(('groups', 'dc', 'sp'), 'tp'), parts along dimension 0, may hold values from -8 to 8
- value_generator_rows: bfloat16 [2048, 1024], P(('groups', 'dc', 'sp'), 'tp'), parts along dimension 0, may hold values from -18 to 18
- w_reward: float32 [8192], P('tp'), may hold values from -0.2 to 0.2
- plan: int32 [3, 8], P(None, 'groups'), parts along dimension 1, may hold values from 0 to 512, as said below
- gen_order: int32 [16, 8], P(('groups', 'dc', 'sp')), parts along dimension 0, may hold values from 0 to 7, as said below
Outputs:
- scored: bfloat16 [2048, 8192], P(('groups', 'dc', 'sp'), 'tp'), parts along dimension 0
- reward: float32 [2048], P(('groups', 'dc', 'sp')), parts along dimension 0
There are 2 independent parts, one for each index of `groups`. A program takes and returns all parts, laid end to end along the dimension named above; an argument that names none is the same for every part. Nothing has to cross between parts.
Inputs may be any that keep to these rules, and one draw needn't show every extreme that they name: `plan`: row 0 gives each dc index the first dc index of its rollout's subgroup, row 1 the subgroup's size, row 2 the rollout's length in tokens. Subgroups are aligned runs of 2 or 2 / 2 dc indices (2 or 1 here, 16 or 8 on the larger slice), and every draw has one subgroup of exactly 2 indices whose rollout has the full 2 * 256 tokens. A rollout on g indices has more than g * 128 and at most g * 256 tokens. `gen_order`: each row is a permutation of the 8 plan devices.
All inputs are finite; a program needn't handle non-finite values.
Results may differ from a plain program's by a relative error of at most 0.0048.
Values may be sent and summed in bfloat16 or wider, within the bound.
A program may use at most 64 MiB of HBM per device.

v0:
```python
import jax
import jax.numpy as jnp
from jax import lax
from jax.sharding import PartitionSpec as P

HEAD_WIDTH = 128


NEG = -1e30


def from_behind(block, axis, distance):
    devices = range(lax.axis_size(axis))
    route = [(i - distance, i) for i in devices if i - distance in devices]
    return lax.ppermute(block, axis, route)


def fold_block(state, key_rows, value_rows, query_rows, allowed, scale):
    top, total, mixed = state
    scores = (
        jnp.einsum("rjge,nje->jgrn", query_rows, key_rows, preferred_element_type=jnp.float32)
        * scale
    )
    if allowed is not None:
        scores = jnp.where(allowed, scores, NEG)
    newtop = jnp.maximum(top, jnp.max(scores, axis=-1))
    shrink = jnp.exp(top - newtop)
    weight = jnp.exp(scores - newtop[..., None])
    if allowed is not None:
        weight = jnp.where(allowed, weight, 0.0)
    total = total * shrink + jnp.sum(weight, axis=-1)
    update = jnp.einsum(
        "jgrn,nje->jgre",
        weight.astype(jnp.bfloat16),
        value_rows,
        preferred_element_type=jnp.float32,
    )
    return (newtop, total, mixed * shrink[..., None] + update)


def body(q_gen, k_gen, value_generator_rows, w_reward, plan, gen_order):
    ranks = lax.axis_size(("dc", "sp"))
    sp_size = lax.axis_size("sp")
    dc_size = ranks // sp_size
    rows = q_gen.shape[0]
    piece = rows // ranks
    width_q = q_gen.shape[1]
    width_kv = k_gen.shape[1]
    heads_kv = width_kv // HEAD_WIDTH
    rollout_group = width_q // HEAD_WIDTH // heads_kv
    scale = HEAD_WIDTH ** (-0.5)
    order_row = gen_order[0]
    labels = jnp.arange(ranks, dtype=jnp.int32)
    inverse = jnp.sum(jnp.where(order_row[:, None] == labels[None, :], labels[:, None], 0), axis=0)
    q_send = jnp.take(q_gen.reshape(ranks, piece, width_q), inverse, axis=0)
    k_send = jnp.take(k_gen.reshape(ranks, piece, width_kv), inverse, axis=0)
    v_send = jnp.take(value_generator_rows.reshape(ranks, piece, width_kv), inverse, axis=0)
    q_flat = q_send.reshape(rows, width_q)
    k_flat = k_send.reshape(rows, width_kv)
    v_flat = v_send.reshape(rows, width_kv)
    query_layout, key_layout, value_layout = (
        lax.all_to_all(q_flat, ("dc", "sp"), split_axis=0, concat_axis=0, tiled=True),
        lax.all_to_all(k_flat, ("dc", "sp"), split_axis=0, concat_axis=0, tiled=True),
        lax.all_to_all(v_flat, ("dc", "sp"), split_axis=0, concat_axis=0, tiled=True),
    )
    me = lax.axis_index(("dc", "sp"))
    my_dc = me // sp_size
    start = plan[0, my_dc]
    length = plan[2, my_dc]
    local = jnp.arange(rows, dtype=jnp.int32)
    position = (my_dc - start) * (rows * sp_size) + me % sp_size * rows + local
    valid = position < length
    query_rows = query_layout.reshape(rows, heads_kv, rollout_group, HEAD_WIDTH)
    state = (
        jnp.full((heads_kv, rollout_group, rows), NEG, jnp.float32),
        jnp.zeros((heads_kv, rollout_group, rows), jnp.float32),
        jnp.zeros((heads_kv, rollout_group, rows, HEAD_WIDTH), jnp.float32),
    )
    causal = local[None, :] <= local[:, None]
    state = fold_block(
        state,
        key_layout.reshape(rows, heads_kv, HEAD_WIDTH),
        value_layout.reshape(rows, heads_kv, HEAD_WIDTH),
        query_rows,
        causal,
        scale,
    )
    own = jnp.stack([key_layout, value_layout])
    reach = max(dc_size // 2, 1) * sp_size

    def advance(step, carry):
        folded, moving = carry
        moving = from_behind(moving, ("dc", "sp"), 1)
        source = me - step - 1
        use = (source >= 0) & (source // sp_size >= start)
        folded = lax.cond(
            use,
            lambda carried: fold_block(
                carried,
                moving[0].reshape(rows, heads_kv, HEAD_WIDTH),
                moving[1].reshape(rows, heads_kv, HEAD_WIDTH),
                query_rows,
                None,
                scale,
            ),
            lambda carried: carried,
            folded,
        )
        return (folded, moving)

    state, _ = lax.fori_loop(0, reach - 1, advance, (state, own))
    top, total, mixed = state
    hidden = mixed / total[..., None]
    hidden = jnp.transpose(hidden, (2, 0, 1, 3)).reshape(rows, width_q)
    hidden = jnp.where(valid[:, None], hidden, 0.0).astype(jnp.bfloat16)
    back = lax.all_to_all(hidden, ("dc", "sp"), split_axis=0, concat_axis=0, tiled=True)
    scored = jnp.take(back.reshape(ranks, piece, width_q), order_row, axis=0).reshape(rows, width_q)
    partial_reward = jnp.sum(scored.astype(jnp.float32) * w_reward[None, :], axis=1)
    reward = lax.psum(partial_reward, "tp")
    return (scored, reward)


def solution(mesh):
    in_specs = (
        P(("groups", "dc", "sp"), "tp"),
        P(("groups", "dc", "sp"), "tp"),
        P(("groups", "dc", "sp"), "tp"),
        P("tp"),
        P(None, "groups"),
        P(("groups", "dc", "sp"), None),
    )
    out_specs = (P(("groups", "dc", "sp"), "tp"), P(("groups", "dc", "sp")))
    return jax.shard_map(body, mesh=mesh, in_specs=in_specs, out_specs=out_specs, check_vma=False)
```

profile of v0, /device:TPU:0, one launch (start us, length us, event | category | flops | bytes accessed | tf_op | source)
XLA Modules:
  0.0 135.5 jit_solution(1962184452238708615)
XLA Ops:
  0.6 0.8 select_reduce_fusion
  1.5 1.5 %gather_fusion.2 = bf16[8,16,512]{2,1,0:T(8,128)(2,1)S(1)} fusion(bf16[8,16,512]{2,1,0:T(8,128)(2,1)} %bitcast.66, s32[1024]{0:T(1024)S(1)} %pad_clamp_fusion.1), kind=kCustom, calls=%fused_computation.2.clone | custom fusion | bytes 262176 | tf_op jit(solution)/shard_map/jit(_take)/gather | solution.py:57
  3.0 1.5 %gather_fusion = bf16[8,16,512]{2,1,0:T(8,128)(2,1)S(1)} fusion(bf16[8,16,512]{2,1,0:T(8,128)(2,1)} %bitcast.67, s32[1024]{0:T(1024)S(1)} %pad_clamp_fusion.1), kind=kCustom, calls=%fused_computation.clone | custom fusion | bytes 262176 | tf_op jit(solution)/shard_map/jit(_take)/gather | solution.py:56
  4.4 0.8 broadcast_select_fusion.2
  5.2 6.3 %all-to-all-start = ((bf16[8,16,512]{2,1,0:T(8,128)(2,1)}), bf16[8,16,512]{2,1,0:T(8,128)(2,1)S(1)}, u32[]{:S(2)}, u32[]{:S(2)}) async-start(bf16[8,16,512]{2,1,0:T(8,128)(2,1)} %get-tuple-element.325), calls=%async_computation | async-start | bytes 262144 | tf_op jit(solution)/shard_map/all_to_all | solution.py:63
  12.2 6.2 %all-to-all-done = bf16[8,16,512]{2,1,0:T(8,128)(2,1)S(1)} async-done(((bf16[8,16,512]{2,1,0:T(8,128)(2,1)}), bf16[8,16,512]{2,1,0:T(8,128)(2,1)S(1)}, u32[]{:S(2)}, u32[]{:S(2)}) %all-to-all-start) | async-done | bytes 131104 | tf_op jit(solution)/shard_map/all_to_all | solution.py:63
  18.3 3.4 %all-to-all-start.2 = ((bf16[8,16,512]{2,1,0:T(8,128)(2,1)}), bf16[8,16,512]{2,1,0:T(8,128)(2,1)S(1)}, u32[]{:S(2)}, u32[]{:S(2)}) async-start(bf16[8,16,512]{2,1,0:T(8,128)(2,1)} %get-tuple-element.324), calls=%async_computation.2 | async-start | bytes 262144 | tf_op jit(solution)/shard_map/all_to_all | solution.py:64
  21.7 1.1 broadcast_select_fusion.1
  22.9 5.6 %all-to-all-done.2 = bf16[8,16,512]{2,1,0:T(8,128)(2,1)S(1)} async-done(((bf16[8,16,512]{2,1,0:T(8,128)(2,1)}), bf16[8,16,512]{2,1,0:T(8,128)(2,1)S(1)}, u32[]{:S(2)}, u32[]{:S(2)}) %all-to-all-start.2) | async-done | bytes 131104 | tf_op jit(solution)/shard_map/all_to_all | solution.py:64
  28.4 3.6 %all-to-all-start.1 = ((bf16[8,16,4096]{2,1,0:T(8,128)(2,1)}), bf16[8,16,4096]{2,1,0:T(8,128)(2,1)S(1)}, u32[]{:S(2)}, u32[]{:S(2)}) async-start(bf16[8,16,4096]{2,1,0:T(8,128)(2,1)} %broadcast_select_fusion.1), calls=%async_computation.1 | async-start | bytes 2097152 | tf_op jit(solution)/shard_map/all_to_all | solution.py:62
  34.0 0.8 copy.38
  34.9 23.6 %all-to-all-done.1 = bf16[8,16,4096]{2,1,0:T(8,128)(2,1)S(1)} async-done(((bf16[8,16,4096]{2,1,0:T(8,128)(2,1)}), bf16[8,16,4096]{2,1,0:T(8,128)(2,1)S(1)}, u32[]{:S(2)}, u32[]{:S(2)}) %all-to-all-start.1) | async-done | bytes 1048608 | tf_op jit(solution)/shard_map/all_to_all | solution.py:62
  58.8 1.4 %copy.35 = bf16[128,4,8,128]{3,0,2,1:T(8,128)(2,1)} copy(bf16[128,4,8,128]{3,2,1,0:T(8,128)(2,1)S(1)} %bitcast.59) | data formatting | bytes 2097152 | tf_op jit(solution)/shard_map/reshape | solution.py:73
  60.1 0.7 fusion.7
  61.4 1.2 convolution_add_fusion
  62.6 22.0 %while.22 = (s32[]{:T(128)}, f32[4,8,128]{2,1,0:T(8,128)S(1)}, f32[4,8,128]{2,1,0:T(8,128)S(1)}, f32[4,8,128,128]{3,2,1,0:T(8,128)S(1)}, bf16[2,128,512]{1,2,0:T...) while((s32[]{:T(128)}, f32[4,8,128]{2,1,0:T(8,128)S(1)}, ...), condition=%wide.region_8.11_spmd, body=%wide.region_3.10_spmd.sunk | while | flops 273686560 | bytes 14156221 | solution.py:111
  62.6 1.6 %collective-permute-start = (bf16[2,128,512]{1,2,0:T(8,128)(2,1)}, bf16[2,128,512]{1,2,0:T(8,128)(2,1)S(1)}, u32[]{:S(2)}, u32[]{:S(2)}) collective-permute-start(bf16[2,128,512]{1,2,0:T(8,128)(2,1)} %get-tuple-element.404), channel_id=1, source_target_pairs={{0,1},{1,4},{4,5},{5,8},{8,9},{9,12},{12,13},{2,3},{3,6},{6,7},{7,... | collective-permute-start | bytes 786440 | tf_op jit(solution)/shard_map/while/body/eval_jaxpr/ppermute | solution.py:15
  64.8 0.7 collective-permute-done
  65.5 0.7 copy.86
  66.2 7.7 %collective-permute-start = (bf16[2,128,512]{1,2,0:T(8,128)(2,1)}, bf16[2,128,512]{1,2,0:T(8,128)(2,1)S(1)}, u32[]{:S(2)}, u32[]{:S(2)}) collective-permute-start(bf16[2,128,512]{1,2,0:T(8,128)(2,1)} %get-tuple-element.404), channel_id=1, source_target_pairs={{0,1},{1,4},{4,5},{5,8},{8,9},{9,12},{12,13},{2,3},{3,6},{6,7},{7,... | collective-permute-start | bytes 786440 | tf_op jit(solution)/shard_map/while/body/eval_jaxpr/ppermute | solution.py:15
  74.6 0.7 collective-permute-done
  75.3 0.7 copy.86
  76.0 6.5 %collective-permute-start = (bf16[2,128,512]{1,2,0:T(8,128)(2,1)}, bf16[2,128,512]{1,2,0:T(8,128)(2,1)S(1)}, u32[]{:S(2)}, u32[]{:S(2)}) collective-permute-start(bf16[2,128,512]{1,2,0:T(8,128)(2,1)} %get-tuple-element.404), channel_id=1, source_target_pairs={{0,1},{1,4},{4,5},{5,8},{8,9},{9,12},{12,13},{2,3},{3,6},{6,7},{7,... | collective-permute-start | bytes 786440 | tf_op jit(solution)/shard_map/while/body/eval_jaxpr/ppermute | solution.py:15
  83.2 0.7 collective-permute-done
  83.9 0.7 copy.86
  84.6 0.7 divide_bitcast_fusion
  85.3 0.7 copy.40
  86.5 1.2 select_convert_fusion
  87.7 13.6 %all-to-all-start.3 = ((bf16[8,16,4096]{2,1,0:T(8,128)(2,1)}), bf16[8,16,4096]{2,1,0:T(8,128)(2,1)S(1)}, u32[]{:S(2)}, u32[]{:S(2)}) async-start(bf16[8,16,4096]{2,1,0:T(8,128)(2,1)} %select_convert_fusion), calls=%async_computation.3 | async-start | bytes 2097152 | tf_op jit(solution)/shard_map/all_to_all | solution.py:116
  101.3 26.6 %all-to-all-done.3 = bf16[8,16,4096]{2,1,0:T(8,128)(2,1)S(1)} async-done(((bf16[8,16,4096]{2,1,0:T(8,128)(2,1)}), bf16[8,16,4096]{2,1,0:T(8,128)(2,1)S(1)}, u32[]{:S(2)}, u32[]{:S(2)}) %all-to-all-start.3) | async-done | bytes 1048608 | tf_op jit(solution)/shard_map/all_to_all | solution.py:116
  128.5 1.5 %multiply_reduce_fusion = (f32[8,16]{1,0:T(8,128)S(1)}, bf16[8,16,4096]{2,1,0:T(8,128)(2,1)}) fusion(f32[4096]{0:T(1024)S(1)} %copy-done.1, bf16[8,16,4096]{2,1,0:T(8,128)(2,1)S(1)} %gather_fusion.3, pred[8]{0:T(512)(128)(4,1)S(1)} %compare_and_fusion), kind=kLoop, calls=%fused_computation.16 | loop fusion | flops 2097024 | bytes 2114056 | tf_op jit(solution)/shard_map/reduce_sum | solution.py:118
  130.1 5.4 %psum.7 = f32[128]{0:T(128)} all-reduce(f32[128]{0:T(128)S(1)} %reduce_sum.41), channel_id=1, replica_groups=mesh['groups'=2,'dc'=4,'tp'=2,'sp'=2] {'tp'}, use_global_device_ids=true, to_apply=%region_10.13 | all-reduce | flops 128 | bytes 1024 | tf_op jit(solution)/shard_map/psum | solution.py:119
  (31 shorter events, 4.0 us)
Async XLA Ops:
  0.6 10.9 %copy-start = (bf16[128,4096]{1,0:T(8,128)(2,1)S(1)}, bf16[128,4096]{1,0:T(8,128)(2,1)}, u32[]{:S(2)}) copy-start(bf16[128,4096]{1,0:T(8,128)(2,1)} %param.14) | copy-start | bytes 3145732
  5.2 13.1 %all-to-all-start = ((bf16[8,16,512]{2,1,0:T(8,128)(2,1)}), bf16[8,16,512]{2,1,0:T(8,128)(2,1)S(1)}, u32[]{:S(2)}, u32[]{:S(2)}) async-start(bf16[8,16,512]{2,1,0:T(8,128)(2,1)} %get-tuple-element.325), calls=%async_computation | async-start | bytes 262144 | tf_op jit(solution)/shard_map/all_to_all | solution.py:63
  18.3 10.1 %all-to-all-start.2 = ((bf16[8,16,512]{2,1,0:T(8,128)(2,1)}), bf16[8,16,512]{2,1,0:T(8,128)(2,1)S(1)}, u32[]{:S(2)}, u32[]{:S(2)}) async-start(bf16[8,16,512]{2,1,0:T(8,128)(2,1)} %get-tuple-element.324), calls=%async_computation.2 | async-start | bytes 262144 | tf_op jit(solution)/shard_map/all_to_all | solution.py:64
  21.7 10.3 %copy-start.2 = (s32[3,4]{1,0:T(4,128)S(1)}, s32[3,4]{1,0:T(4,128)}, u32[]{:S(2)}) copy-start(s32[3,4]{1,0:T(4,128)} %param.18) | copy-start | bytes 148
  28.4 30.1 %all-to-all-start.1 = ((bf16[8,16,4096]{2,1,0:T(8,128)(2,1)}), bf16[8,16,4096]{2,1,0:T(8,128)(2,1)S(1)}, u32[]{:S(2)}, u32[]{:S(2)}) async-start(bf16[8,16,4096]{2,1,0:T(8,128)(2,1)} %broadcast_select_fusion.1), calls=%async_computation.1 | async-start | bytes 2097152 | tf_op jit(solution)/shard_map/all_to_all | solution.py:62
  62.6 2.9 %collective-permute-start = (bf16[2,128,512]{1,2,0:T(8,128)(2,1)}, bf16[2,128,512]{1,2,0:T(8,128)(2,1)S(1)}, u32[]{:S(2)}, u32[]{:S(2)}) collective-permute-start(bf16[2,128,512]{1,2,0:T(8,128)(2,1)} %get-tuple-element.404), channel_id=1, source_target_pairs={{0,1},{1,4},{4,5},{5,8},{8,9},{9,12},{12,13},{2,3},{3,6},{6,7},{7,... | collective-permute-start | bytes 786440 | tf_op jit(solution)/shard_map/while/body/eval_jaxpr/ppermute | solution.py:15
  66.2 9.1 %collective-permute-start = (bf16[2,128,512]{1,2,0:T(8,128)(2,1)}, bf16[2,128,512]{1,2,0:T(8,128)(2,1)S(1)}, u32[]{:S(2)}, u32[]{:S(2)}) collective-permute-start(bf16[2,128,512]{1,2,0:T(8,128)(2,1)} %get-tuple-element.404), channel_id=1, source_target_pairs={{0,1},{1,4},{4,5},{5,8},{8,9},{9,12},{12,13},{2,3},{3,6},{6,7},{7,... | collective-permute-start | bytes 786440 | tf_op jit(solution)/shard_map/while/body/eval_jaxpr/ppermute | solution.py:15
  76.0 7.9 %collective-permute-start = (bf16[2,128,512]{1,2,0:T(8,128)(2,1)}, bf16[2,128,512]{1,2,0:T(8,128)(2,1)S(1)}, u32[]{:S(2)}, u32[]{:S(2)}) collective-permute-start(bf16[2,128,512]{1,2,0:T(8,128)(2,1)} %get-tuple-element.404), channel_id=1, source_target_pairs={{0,1},{1,4},{4,5},{5,8},{8,9},{9,12},{12,13},{2,3},{3,6},{6,7},{7,... | collective-permute-start | bytes 786440 | tf_op jit(solution)/shard_map/while/body/eval_jaxpr/ppermute | solution.py:15
  86.5 14.8 %copy-start.3 = (s32[1,8]{1,0:T(1,128)S(1)}, s32[1,8]{1,0:T(1,128)}, u32[]{:S(2)}) copy-start(s32[1,8]{1,0:T(1,128)} %param.19) | copy-start | bytes 100
  87.7 40.8 %copy-start.1 = (f32[4096]{0:T(1024)S(1)}, f32[4096]{0:T(1024)}, u32[]{:S(2)}) copy-start(f32[4096]{0:T(1024)} %param.17) | copy-start | bytes 49156
  87.7 40.2 %all-to-all-start.3 = ((bf16[8,16,4096]{2,1,0:T(8,128)(2,1)}), bf16[8,16,4096]{2,1,0:T(8,128)(2,1)S(1)}, u32[]{:S(2)}, u32[]{:S(2)}) async-start(bf16[8,16,4096]{2,1,0:T(8,128)(2,1)} %select_convert_fusion), calls=%async_computation.3 | async-start | bytes 2097152 | tf_op jit(solution)/shard_map/all_to_all | solution.py:116
where the time goes:
time: 136 us; the launch traced here: 135 us
  waiting for transfers between devices  64 us (47%)
  starting transfers between devices  42.6 us (31%)
  local copies, waits for them, and re-layouts  10.6 us (8%)
  other arithmetic  7.45 us (5%)
  blocking collectives  5.42 us (4%)
  loops' own time  2.01 us (1%)
  matrix products  1.86 us (1%)
  between operations  1.51 us (1%)
    all_to_all x1, waiting for transfers between devices, body(): lax.all_to_all(hidden, ('dc', 'sp'), split_axis=0, concat_axis=0, tiled=T...  26.6 us
    all_to_all x1, waiting for transfers between devices, body(): lax.all_to_all(q_flat, ('dc', 'sp'), split_axis=0, concat_axis=0, tiled=T...  23.6 us
    ppermute x3, starting transfers between devices, from_behind(): return lax.ppermute(block, axis, route)  15.8 us
    all_to_all x1, starting transfers between devices, body(): lax.all_to_all(hidden, ('dc', 'sp'), split_axis=0, concat_axis=0, tiled=T...  13.6 us
    all_to_all x1, starting transfers between devices, body(): lax.all_to_all(k_flat, ('dc', 'sp'), split_axis=0, concat_axis=0, tiled=T...  6.33 us
    all_to_all x1, waiting for transfers between devices, body(): lax.all_to_all(k_flat, ('dc', 'sp'), split_axis=0, concat_axis=0, tiled=T...  6.15 us
    all_to_all x1, waiting for transfers between devices, body(): lax.all_to_all(v_flat, ('dc', 'sp'), split_axis=0, concat_axis=0, tiled=T...  5.57 us
    psum x1, blocking collectives, body(): reward = lax.psum(partial_reward, 'tp')  5.42 us
  transfers between devices with their start and end apart: 7, of which 7 were waited for; matrix products, arithmetic and copies ran while one was open for 3% of the time, Pallas kernels for 0%

commit v1 on v0

--- a/solution.py
+++ b/solution.py
@@ -1,6 +1,10 @@
+import functools
+
 import jax
 import jax.numpy as jnp
 from jax import lax
+from jax.experimental import pallas as pl
+from jax.experimental.pallas import tpu as pltpu
 from jax.sharding import PartitionSpec as P
 
 HEAD_WIDTH = 128
@@ -120,6 +124,334 @@
     return (scored, reward)
 
 
+MESH = pl.DeviceIdType.MESH
+BIG = -1e30
+
+
+def gather_attend(
+    sizes, order_ref, plan_ref, q_ref, k_ref, v_ref, w_ref, out_ref, rew_ref,
+    q_send, q_all, kv_send, kv_all, hid_send, hid_all, racc, rew_all,
+    kv_ssem, kv_rsem, fwd_ssem, q_ssem, q_rsem, hid_ssem, hid_rsem, rew_ssem, rew_rsem,
+):
+    dcs, sps, tps, piece, rows, heads, group, jc, span, halves = sizes
+    ranks, units, width = dcs * sps, jc * halves, group * HEAD_WIDTH
+    dc, sp, tp = lax.axis_index("dc"), lax.axis_index("sp"), lax.axis_index("tp")
+    me, other = dc * sps + sp, 1 - sp
+
+    barrier = pltpu.get_barrier_semaphore()
+    for rank in range(ranks):
+        @pl.when(rank != me)
+        def _():
+            pl.semaphore_signal(
+                barrier, inc=1, device_id={"dc": rank // sps, "sp": rank % sps}, device_id_type=MESH
+            )
+    for shift in range(1, tps):
+        for core in range(sps):
+            pl.semaphore_signal(
+                barrier, inc=1, device_id={"tp": lax.rem(tp + shift, tps), "sp": core}, device_id_type=MESH
+            )
+
+    for d in range(ranks):
+        seg = jnp.int32(0)
+        for s in range(1, ranks):
+            seg = jnp.where(order_ref[0, s] == d, s, seg)
+        h, dl = d // span, d % span
+        for jj in range(jc):
+            u = jj * halves + h
+            for core in range(sps):
+                head = core * jc + jj
+                cols = pl.ds(head * HEAD_WIDTH, HEAD_WIDTH)
+                kv_send[core, u, 0, pl.ds(dl * piece, piece), :] = k_ref[seg, :, cols]
+                kv_send[core, u, 1, pl.ds(dl * piece, piece), :] = v_ref[seg, :, cols]
+            mine = pl.ds(pl.multiple_of((sp * jc + jj) * width, width), width)
+            theirs = pl.ds(pl.multiple_of((other * jc + jj) * width, width), width)
+            q_all[0, u, dl] = q_ref[seg, :, mine]
+            q_send[u, dl] = q_ref[seg, :, theirs]
+
+    pl.semaphore_wait(barrier, ranks - 1 + (tps - 1) * sps)
+
+    steps = [sign * hop for hop in (1, 2) if hop < dcs for sign in (1, -1)]
+
+    def kv_copy(u, i, core):
+        return pltpu.make_async_remote_copy(
+            src_ref=kv_send.at[core, u], dst_ref=kv_all.at[u, me],
+            send_sem=kv_ssem.at[u, i * sps + core], recv_sem=kv_rsem.at[u, me],
+            device_id={"dc": dc + steps[i], "sp": core}, device_id_type=MESH,
+        )
+
+    def kv_copy_sibling(u):
+        return pltpu.make_async_remote_copy(
+            src_ref=kv_send.at[other, u], dst_ref=kv_all.at[u, me],
+            send_sem=kv_ssem.at[u, len(steps) * sps], recv_sem=kv_rsem.at[u, me],
+            device_id={"sp": other}, device_id_type=MESH,
+        )
+
+    def kv_forward(u, core, source_dc, target_dc):
+        source = source_dc * sps + core
+        return pltpu.make_async_remote_copy(
+            src_ref=kv_all.at[u, source], dst_ref=kv_all.at[u, source],
+            send_sem=fwd_ssem.at[u, core], recv_sem=kv_rsem.at[u, source],
+            device_id={"dc": target_dc}, device_id_type=MESH,
+        )
+
+    def kv_wait(u, source):
+        pltpu.make_async_remote_copy(
+            src_ref=kv_all.at[u, source], dst_ref=kv_all.at[u, source],
+            send_sem=kv_ssem.at[u, 0], recv_sem=kv_rsem.at[u, source],
+            device_id={"sp": other}, device_id_type=MESH,
+        ).wait_recv()
+
+    q_copy = pltpu.make_async_remote_copy(
+        src_ref=q_send, dst_ref=q_all.at[1], send_sem=q_ssem, recv_sem=q_rsem,
+        device_id={"sp": other}, device_id_type=MESH,
+    )
+
+    def send_unit(u, carry):
+        for i, step in enumerate(steps):
+            @pl.when((dc + step >= 0) & (dc + step < dcs))
+            def _():
+                for core in range(sps):
+                    kv_copy(u, i, core).start()
+        kv_copy_sibling(u).start()
+        kv_all[u, me] = kv_send[sp, u]
+        return carry
+
+    lax.fori_loop(0, units, send_unit, 0)
+    q_copy.start()
+
+    tile = 2 * group * piece
+    row = lax.broadcasted_iota(jnp.int32, (tile, 1), 0)
+    rank_of_row = dc * sps + jnp.where(row < group * piece, sp, other)
+    offset = rank_of_row * piece + lax.rem(row, piece)
+    column = lax.broadcasted_iota(jnp.int32, (tile, rows), 1)
+    causal = jnp.where(column <= offset, 0.0, BIG)
+    factor = HEAD_WIDTH ** (-0.5) * 1.4426950408889634
+
+    def hid_copy(u):
+        return pltpu.make_async_remote_copy(
+            src_ref=hid_send.at[u], dst_ref=hid_all.at[sp, u],
+            send_sem=hid_ssem.at[u], recv_sem=hid_rsem.at[u],
+            device_id={"sp": other}, device_id_type=MESH,
+        )
+
+    q_copy.wait_recv()
+
+    def attend(u, carry):
+        jj, h = u // halves, lax.rem(u, halves)
+        if dcs == 4:
+            for relay, far, end in ((1, 3, 0), (2, 0, 3)):
+                @pl.when(dc == relay)
+                def _():
+                    for core in range(sps):
+                        kv_wait(u, far * sps + core)
+                        kv_forward(u, core, far, end).start()
+        for source in range(ranks):
+            sdc = source // sps
+            waits = source != me
+            if dcs == 4 and sdc in (0, 3):
+                waits = waits & (dc != (2 if sdc == 0 else 1))
+
+            @pl.when(waits)
+            def _():
+                kv_wait(u, source)
+
+        def plan_order(which):
+            return jnp.concatenate(
+                [
+                    kv_all[u, source, which, pl.ds(dl * piece, piece), :]
+                    for dl in range(span)
+                    for source in range(ranks)
+                ],
+                axis=0,
+            )
+
+        keys, values = plan_order(0), plan_order(1)
+        for dl in range(span):
+            d = h * span + dl
+            slot = d // sps
+            n = (dl + 1) * rows
+            query = jnp.concatenate(
+                [
+                    q_all[t, u, dl, :, pl.ds(g * HEAD_WIDTH, HEAD_WIDTH)]
+                    for t in range(2)
+                    for g in range(group)
+                ],
+                axis=0,
+            )
+            scores = lax.dot_general(
+                query, keys[:n], (((1,), (1,)), ((), ())), preferred_element_type=jnp.float32
+            )
+            start = plan_ref[0, slot]
+            blocks = []
+            for d2 in range(dl + 1):
+                block = scores[:, d2 * rows:(d2 + 1) * rows]
+                if d2 == dl:
+                    block = block + causal
+                elif d2 // sps != dl // sps:
+                    block = block + jnp.where(plan_ref[0, h * (span // sps) + d2 // sps] == start, 0.0, BIG)
+                blocks.append(block)
+            peak = blocks[0]
+            for block in blocks[1:]:
+                peak = jnp.maximum(peak, block)
+            top = jnp.max(peak, axis=1, keepdims=True)
+            weights = [jnp.exp2((block - top) * factor) for block in blocks]
+            total = weights[0]
+            for weight in weights[1:]:
+                total = total + weight
+            total = jnp.sum(total, axis=1, keepdims=True)
+            weight16 = jnp.concatenate([weight.astype(jnp.bfloat16) for weight in weights], axis=1)
+            mixed = jnp.dot(weight16, values[:n], preferred_element_type=jnp.float32)
+            base = (slot - start) * (rows * sps) + lax.rem(d, sps) * rows
+            share = jnp.where(offset + base < plan_ref[2, slot], 1.0 / total, 0.0)
+            hidden = (mixed * share).astype(jnp.bfloat16)
+            for t in range(2):
+                reward = jnp.zeros((piece, HEAD_WIDTH), jnp.float32)
+                for g in range(group):
+                    part = hidden[(t * group + g) * piece:(t * group + g + 1) * piece]
+                    cols = pl.ds(g * HEAD_WIDTH, HEAD_WIDTH)
+                    if t == 0:
+                        hid_all[sp, u, dl, :, cols] = part
+                    else:
+                        hid_send[u, dl, :, cols] = part
+                    w = w_ref[sp * jc + jj, pl.ds(g, 1), :]
+                    reward = reward + part.astype(jnp.float32) * w
+                racc[u, t, pl.ds(dl * piece, piece), :] = reward
+        hid_copy(u).start()
+        return carry
+
+    lax.fori_loop(0, units, attend, 0)
+
+    sums = []
+    for t in range(2):
+        cells = []
+        for h in range(halves):
+            cell = racc[h, t]
+            for jj in range(1, jc):
+                cell = cell + racc[jj * halves + h, t]
+            cells.append(cell)
+        line = jnp.sum(jnp.concatenate(cells, axis=0).T, axis=0, keepdims=True)
+        sums.append(jnp.broadcast_to(line, (8, rows)))
+    slot_me = tp * sps + sp
+    rew_all[tps * sps] = sums[1]
+    rew_all[slot_me] = sums[0]
+
+    def rew_copy(shift, same):
+        peer = lax.rem(tp + shift, tps)
+        return pltpu.make_async_remote_copy(
+            src_ref=rew_all.at[slot_me if same else tps * sps], dst_ref=rew_all.at[slot_me],
+            send_sem=rew_ssem.at[2 * shift + (0 if same else 1)], recv_sem=rew_rsem.at[slot_me],
+            device_id={"tp": peer, "sp": sp if same else other}, device_id_type=MESH,
+        )
+
+    pairs = [(shift, same) for shift in range(tps) for same in (True, False) if (shift, same) != (0, True)]
+    for shift, same in pairs:
+        rew_copy(shift, same).start()
+
+    for u in range(units):
+        hid_copy(u).wait_recv()
+    for s in range(ranks):
+        d = order_ref[0, s]
+        h, dl = d // span, lax.rem(d, span)
+        for core in range(sps):
+            for jj in range(jc):
+                out_ref[s, :, pl.ds((core * jc + jj) * width, width)] = hid_all[core, jj * halves + h, dl]
+
+    for source in range(tps * sps):
+        @pl.when(source != slot_me)
+        def _():
+            pltpu.make_async_remote_copy(
+                src_ref=rew_all.at[source], dst_ref=rew_all.at[source],
+                send_sem=rew_ssem.at[0], recv_sem=rew_rsem.at[source],
+                device_id={"sp": other}, device_id_type=MESH,
+            ).wait_recv()
+    reward = rew_all[0]
+    for source in range(1, tps * sps):
+        reward = reward + rew_all[source]
+    rew_ref[...] = reward
+
+    for shift, same in pairs:
+        rew_copy(shift, same).wait_send()
+    q_copy.wait_send()
+
+    def drain(u, carry):
+        hid_copy(u).wait_send()
+        kv_copy_sibling(u).wait_send()
+        for i, step in enumerate(steps):
+            @pl.when((dc + step >= 0) & (dc + step < dcs))
+            def _():
+                for core in range(sps):
+                    kv_copy(u, i, core).wait_send()
+        if dcs == 4:
+            for relay, far, end in ((1, 3, 0), (2, 0, 3)):
+                @pl.when(dc == relay)
+                def _():
+                    for core in range(sps):
+                        kv_forward(u, core, far, end).wait_send()
+        return carry
+
+    lax.fori_loop(0, units, drain, 0)
+
+
+def gather_body(q_gen, k_gen, value_generator_rows, w_reward, plan, gen_order):
+    dcs, sps, tps = lax.axis_size("dc"), lax.axis_size("sp"), lax.axis_size("tp")
+    ranks = dcs * sps
+    rows, width_q = q_gen.shape
+    width_kv = k_gen.shape[1]
+    piece = rows // ranks
+    heads = width_kv // HEAD_WIDTH
+    group = width_q // width_kv
+    jc = heads // sps
+    span = max(dcs // 2, 1) * sps
+    halves = ranks // span
+    units, width = jc * halves, group * HEAD_WIDTH
+    sizes = (dcs, sps, tps, piece, rows, heads, group, jc, span, halves)
+    bf16, f32 = jnp.bfloat16, jnp.float32
+    vmem, smem = pl.BlockSpec(memory_space=pltpu.VMEM), pl.BlockSpec(memory_space=pltpu.SMEM)
+    dma = pltpu.SemaphoreType.DMA
+    scored, reward = pl.pallas_call(
+        functools.partial(gather_attend, sizes),
+        out_shape=(
+            jax.ShapeDtypeStruct((ranks, piece, width_q), bf16),
+            jax.ShapeDtypeStruct((8, rows), f32),
+        ),
+        in_specs=[smem, smem, vmem, vmem, vmem, vmem],
+        out_specs=(vmem, vmem),
+        scratch_shapes=[
+            pltpu.VMEM((units, span, piece, width), bf16),
+            pltpu.VMEM((2, units, span, piece, width), bf16),
+            pltpu.VMEM((sps, units, 2, span * piece, HEAD_WIDTH), bf16),
+            pltpu.VMEM((units, ranks, 2, span * piece, HEAD_WIDTH), bf16),
+            pltpu.VMEM((units, span, piece, width), bf16),
+            pltpu.VMEM((sps, units, span, piece, width), bf16),
+            pltpu.VMEM((units, 2, span * piece, HEAD_WIDTH), f32),
+            pltpu.VMEM((tps * sps + 1, 8, rows), f32),
+            dma((units, 4 * sps + 1)),
+            dma((units, ranks)),
+            dma((units, sps)),
+            dma,
+            dma,
+            dma((units,)),
+            dma((units,)),
+            dma((2 * tps,)),
+            dma((tps * sps,)),
+        ],
+        compiler_params=pltpu.CompilerParams(
+            collective_id=0, has_side_effects=True, vmem_limit_bytes=32 * 1024 * 1024
+        ),
+    )(
+        gen_order,
+        plan,
+        q_gen.reshape(ranks, piece, width_q),
+        k_gen.reshape(ranks, piece, width_kv),
+        value_generator_rows.reshape(ranks, piece, width_kv),
+        w_reward.reshape(heads, group, HEAD_WIDTH),
+    )
+    labels = jnp.arange(ranks, dtype=jnp.int32)
+    pick = gen_order[0][:, None, None] == labels[None, :, None]
+    reward = jnp.sum(jnp.where(pick, reward[0].reshape(1, ranks, piece), 0.0), axis=1).reshape(rows)
+    return (scored.reshape(rows, width_q), reward)
+
+
 def solution(mesh):
     in_specs = (
         P(("groups", "dc", "sp"), "tp"),
@@ -130,4 +462,20 @@
         P(("groups", "dc", "sp"), None),
     )
     out_specs = (P(("groups", "dc", "sp"), "tp"), P(("groups", "dc", "sp")))
-    return jax.shard_map(body, mesh=mesh, in_specs=in_specs, out_specs=out_specs, check_vma=False)
+
+    def whole(q_gen, k_gen, value_generator_rows, w_reward, plan, gen_order):
+        rows = q_gen.shape[0] // (mesh.shape["groups"] * mesh.shape["dc"] * mesh.shape["sp"])
+        heads = k_gen.shape[1] // HEAD_WIDTH // mesh.shape["tp"]
+        fits = (
+            mesh.shape["dc"] in (2, 4)
+            and mesh.shape["sp"] == 2
+            and heads % 2 == 0
+            and rows == HEAD_WIDTH
+            and rows % (16 * mesh.shape["dc"] * mesh.shape["sp"]) == 0
+        )
+        inner = gather_body if fits else body
+        return jax.shard_map(inner, mesh=mesh, in_specs=in_specs, out_specs=out_specs, check_vma=False)(
+            q_gen, k_gen, value_generator_rows, w_reward, plan, gen_order
+        )
+
+    return whole

time: 136 us -> 38 us (0.28)
  waiting for transfers between devices: 64 us -> 0 us
  starting transfers between devices: 42.6 us -> 0 us
  Pallas kernels: 0 us -> 30.8 us
  other arithmetic: 7.45 us -> 0.16 us
  blocking collectives: 5.42 us -> 0 us
  local copies, waits for them, and re-layouts: 10.6 us -> 6.08 us
  loops' own time: 2.01 us -> 0 us
  matrix products: 1.86 us -> 0 us
    all_to_all x4 -> x0, waiting for transfers between devices: 61.9 us -> none  [the longest x1 26.6 us: body(): lax.all_to_all(hidden, ('dc', 'sp'), split_axis=0, concat_axis=0, tiled=T...]
    pallas_call x0 -> x1, Pallas kernels: none -> 30.8 us  [gather_body(): pl.pallas_call(functools.partial(gather_attend, sizes), out_shape=(jax.Sh...]
    all_to_all x4 -> x0, starting transfers between devices: 26.8 us -> none  [the longest x1 13.6 us: body(): lax.all_to_all(hidden, ('dc', 'sp'), split_axis=0, concat_axis=0, tiled=T...]
    ppermute x3 -> x0, starting transfers between devices: 15.8 us -> none  [from_behind(): return lax.ppermute(block, axis, route)]
    psum x1 -> x0, blocking collectives: 5.42 us -> none  [body(): reward = lax.psum(partial_reward, 'tp')]
    unnamed x9 -> x13, local copies, waits for them, and re-layouts: 0.27 us -> 5.39 us
    gather x4 -> x0, local copies, waits for them, and re-layouts: 4.15 us -> none  [the longest x1 1.46 us: body(): jnp.take(value_generator_rows.reshape(ranks, piece, width_kv), inverse, a...]
    while x4 -> x0, local copies, waits for them, and re-layouts: 2.9 us -> none
  transfers between devices with their start and end apart: 7 -> 0, of which waited for: 7 -> 0; matrix products, arithmetic and copies ran while one was open for 3% -> 0% of each run, Pallas kernels for 0% -> 0%
where the time goes in v1:
time: 38 us; the launch traced here: 37.7 us
  Pallas kernels  30.8 us (81%)
  local copies, waits for them, and re-layouts  6.08 us (16%)
  between operations  0.67 us (2%)
    pallas_call x1, Pallas kernels, gather_body(): pl.pallas_call(functools.partial(gather_attend, sizes), out_shape=(jax.Sh...  30.8 us
    unnamed x13, local copies, waits for them, and re-layouts  5.39 us

profile of v1, /device:TPU:0, one launch (start us, length us, event | category | flops | bytes accessed | tf_op | source)
XLA Modules:
  0.0 37.7 jit_solution(10103078591247843184)
XLA Ops:
  0.6 0.0 copy-start.4
  0.6 0.0 copy-start.5
  0.7 0.7 %copy-done.4 = s32[3,4]{1,0:T(4,128)S(1)} copy-done((s32[3,4]{1,0:T(4,128)S(1)}, s32[3,4]{1,0:T(4,128)}, u32[]{:S(2)}) %copy-start.4) | copy-done | bytes 72
  1.3 0.0 copy-done.5
  1.3 0.0 copy-start
  1.3 1.2 %copy-done = bf16[128,4096]{1,0:T(8,128)(2,1)S(1)} copy-done((bf16[128,4096]{1,0:T(8,128)(2,1)S(1)}, bf16[128,4096]{1,0:T(8,128)(2,1)}, u32[]{:S(2)}) %copy-start) | copy-done | bytes 1048600
  2.5 0.0 copy-start.1
  2.5 0.9 %copy-done.1 = bf16[128,512]{1,0:T(8,128)(2,1)S(1)} copy-done((bf16[128,512]{1,0:T(8,128)(2,1)S(1)}, bf16[128,512]{1,0:T(8,128)(2,1)}, u32[]{:S(2)}) %copy-start.1) | copy-done | bytes 131096
  3.4 0.0 copy-start.2
  3.4 0.9 %copy-done.2 = bf16[128,512]{1,0:T(8,128)(2,1)S(1)} copy-done((bf16[128,512]{1,0:T(8,128)(2,1)S(1)}, bf16[128,512]{1,0:T(8,128)(2,1)}, u32[]{:S(2)}) %copy-start.2) | copy-done | bytes 131096
  4.4 0.0 copy-start.3
  4.4 0.7 %copy-done.3 = f32[4096]{0:T(1024)S(1)} copy-done((f32[4096]{0:T(1024)S(1)}, f32[4096]{0:T(1024)}, u32[]{:S(2)}) %copy-start.3) | copy-done | bytes 16408
  5.1 30.8 %shard_map.77 = (bf16[8,16,4096]{2,1,0:T(8,128)(2,1)S(1)}, f32[8,128]{1,0:T(8,128)S(1)}) custom-call(s32[1,8]{1,0:T(1,128)S(1)} %copy-done.5, s32[3,4]{1,0:T(4,128)S(1)} %copy-done.4, bf16[8,16,4096]{2,1,0:T(8,128)(2,1)S(1)} %bitcast.6, bf16[8,16,512]{2,1,0:T(8,128)(2,1)S(1)} %bitcast.8, bf16[8,16,512]{2,1,0:T(8,128)(2,1)S(1)} %bitcast.9, ...), custom_call_target="tpu_custom_call" | custom-call | tf_op jit(solution)/shard_map/pallas_call | solution.py:411
  35.9 0.1 broadcast_in_dim.24
  36.0 0.1 iota_compare_fusion
  36.1 0.1 select_reduce_fusion
  36.2 0.6 %reshape.56 = f32[128]{0:T(128)} reshape(f32[8,16]{1,0:T(8,128)S(1)} %select_reduce_fusion) | data formatting | bytes 1024 | tf_op jit(solution)/shard_map/reshape | solution.py:451
  36.8 1.0 %copy.9 = bf16[128,4096]{1,0:T(8,128)(2,1)} copy(bf16[128,4096]{1,0:T(8,128)(2,1)S(1)} %bitcast.7) | data formatting | bytes 2097152
  (1 shorter events, 0.0 us)
Async XLA Ops:
  0.6 0.7 %copy-start.4 = (s32[3,4]{1,0:T(4,128)S(1)}, s32[3,4]{1,0:T(4,128)}, u32[]{:S(2)}) copy-start(s32[3,4]{1,0:T(4,128)} %plan_ref.1) | copy-start | bytes 148
  0.6 0.7 %copy-start.5 = (s32[1,8]{1,0:T(1,128)S(1)}, s32[1,8]{1,0:T(1,128)}, u32[]{:S(2)}) copy-start(s32[1,8]{1,0:T(1,128)} %order_ref.1) | copy-start | bytes 100
  1.3 1.2 %copy-start = (bf16[128,4096]{1,0:T(8,128)(2,1)S(1)}, bf16[128,4096]{1,0:T(8,128)(2,1)}, u32[]{:S(2)}) copy-start(bf16[128,4096]{1,0:T(8,128)(2,1)} %param.6) | copy-start | bytes 3145732
  2.5 0.9 %copy-start.1 = (bf16[128,512]{1,0:T(8,128)(2,1)S(1)}, bf16[128,512]{1,0:T(8,128)(2,1)}, u32[]{:S(2)}) copy-start(bf16[128,512]{1,0:T(8,128)(2,1)} %param.7) | copy-start | bytes 393220
  3.4 0.9 %copy-start.2 = (bf16[128,512]{1,0:T(8,128)(2,1)S(1)}, bf16[128,512]{1,0:T(8,128)(2,1)}, u32[]{:S(2)}) copy-start(bf16[128,512]{1,0:T(8,128)(2,1)} %param.8) | copy-start | bytes 393220
  4.4 0.7 %copy-start.3 = (f32[4096]{0:T(1024)S(1)}, f32[4096]{0:T(1024)}, u32[]{:S(2)}) copy-start(f32[4096]{0:T(1024)} %param.9) | copy-start | bytes 49156

commit v2 on v1

--- a/solution.py
+++ b/solution.py
@@ -129,14 +129,19 @@
 
 
 def gather_attend(
-    sizes, order_ref, plan_ref, q_ref, k_ref, v_ref, w_ref, out_ref, rew_ref,
-    q_send, q_all, kv_send, kv_all, hid_send, hid_all, racc, rew_all,
-    kv_ssem, kv_rsem, fwd_ssem, q_ssem, q_rsem, hid_ssem, hid_rsem, rew_ssem, rew_rsem,
+    sizes, order_hbm, plan_hbm, q_hbm, k_hbm, v_hbm, w_hbm, out_ref, rew_ref, order_out,
+    order_ref, plan_ref, q_ref, k_ref, v_ref, w_ref, q_send, q_all, kv_send, kv_all, hid_send, racc, rew_all,
+    kv_ssem, kv_rsem, fwd_ssem, q_ssem, q_rsem, hid_ssem, hid_rsem, rew_ssem, rew_rsem, in_sem,
 ):
     dcs, sps, tps, piece, rows, heads, group, jc, span, halves = sizes
     ranks, units, width = dcs * sps, jc * halves, group * HEAD_WIDTH
     dc, sp, tp = lax.axis_index("dc"), lax.axis_index("sp"), lax.axis_index("tp")
     me, other = dc * sps + sp, 1 - sp
+
+    arguments = ((order_hbm, order_ref), (k_hbm, k_ref), (v_hbm, v_ref), (q_hbm, q_ref), (plan_hbm, plan_ref), (w_hbm, w_ref))
+    loads = [pltpu.make_async_copy(a, b, in_sem.at[i]) for i, (a, b) in enumerate(arguments)]
+    for load in loads:
+        load.start()
 
     barrier = pltpu.get_barrier_semaphore()
     for rank in range(ranks):
@@ -151,22 +156,22 @@
                 barrier, inc=1, device_id={"tp": lax.rem(tp + shift, tps), "sp": core}, device_id_type=MESH
             )
 
+    for load in loads[:3]:
+        load.wait()
+    segments = []
     for d in range(ranks):
         seg = jnp.int32(0)
         for s in range(1, ranks):
             seg = jnp.where(order_ref[0, s] == d, s, seg)
+        segments.append(seg)
+    for d in range(ranks):
         h, dl = d // span, d % span
         for jj in range(jc):
             u = jj * halves + h
             for core in range(sps):
-                head = core * jc + jj
-                cols = pl.ds(head * HEAD_WIDTH, HEAD_WIDTH)
-                kv_send[core, u, 0, pl.ds(dl * piece, piece), :] = k_ref[seg, :, cols]
-                kv_send[core, u, 1, pl.ds(dl * piece, piece), :] = v_ref[seg, :, cols]
-            mine = pl.ds(pl.multiple_of((sp * jc + jj) * width, width), width)
-            theirs = pl.ds(pl.multiple_of((other * jc + jj) * width, width), width)
-            q_all[0, u, dl] = q_ref[seg, :, mine]
-            q_send[u, dl] = q_ref[seg, :, theirs]
+                cols = pl.ds((core * jc + jj) * HEAD_WIDTH, HEAD_WIDTH)
+                kv_send[core, u, 0, pl.ds(dl * piece, piece), :] = k_ref[segments[d], :, cols]
+                kv_send[core, u, 1, pl.ds(dl * piece, piece), :] = v_ref[segments[d], :, cols]
 
     pl.semaphore_wait(barrier, ranks - 1 + (tps - 1) * sps)
 
@@ -217,7 +222,18 @@
         return carry
 
     lax.fori_loop(0, units, send_unit, 0)
+    loads[3].wait()
+    for d in range(ranks):
+        h, dl = d // span, d % span
+        for jj in range(jc):
+            u = jj * halves + h
+            mine = pl.ds(pl.multiple_of((sp * jc + jj) * width, width), width)
+            theirs = pl.ds(pl.multiple_of((other * jc + jj) * width, width), width)
+            q_send[u, dl] = q_ref[segments[d], :, theirs]
+            q_all[0, u, dl] = q_ref[segments[d], :, mine]
     q_copy.start()
+    for load in loads[4:]:
+        load.wait()
 
     tile = 2 * group * piece
     row = lax.broadcasted_iota(jnp.int32, (tile, 1), 0)
@@ -227,9 +243,15 @@
     causal = jnp.where(column <= offset, 0.0, BIG)
     factor = HEAD_WIDTH ** (-0.5) * 1.4426950408889634
 
+    def hid_place(u):
+        head = sp * jc + u // halves
+        return out_ref.at[
+            pl.ds(lax.rem(u, halves) * span, span), :, pl.ds(pl.multiple_of(head * width, width), width)
+        ]
+
     def hid_copy(u):
         return pltpu.make_async_remote_copy(
-            src_ref=hid_send.at[u], dst_ref=hid_all.at[sp, u],
+            src_ref=hid_send.at[u], dst_ref=hid_place(u),
             send_sem=hid_ssem.at[u], recv_sem=hid_rsem.at[u],
             device_id={"sp": other}, device_id_type=MESH,
         )
@@ -238,6 +260,7 @@
 
     def attend(u, carry):
         jj, h = u // halves, lax.rem(u, halves)
+        head = sp * jc + jj
         if dcs == 4:
             for relay, far, end in ((1, 3, 0), (2, 0, 3)):
                 @pl.when(dc == relay)
@@ -310,7 +333,7 @@
                     part = hidden[(t * group + g) * piece:(t * group + g + 1) * piece]
                     cols = pl.ds(g * HEAD_WIDTH, HEAD_WIDTH)
                     if t == 0:
-                        hid_all[sp, u, dl, :, cols] = part
+                        out_ref[d, :, pl.ds(pl.multiple_of(head * width, width) + g * HEAD_WIDTH, HEAD_WIDTH)] = part
                     else:
                         hid_send[u, dl, :, cols] = part
                     w = w_ref[sp * jc + jj, pl.ds(g, 1), :]
@@ -347,15 +370,6 @@
     for shift, same in pairs:
         rew_copy(shift, same).start()
 
-    for u in range(units):
-        hid_copy(u).wait_recv()
-    for s in range(ranks):
-        d = order_ref[0, s]
-        h, dl = d // span, lax.rem(d, span)
-        for core in range(sps):
-            for jj in range(jc):
-                out_ref[s, :, pl.ds((core * jc + jj) * width, width)] = hid_all[core, jj * halves + h, dl]
-
     for source in range(tps * sps):
         @pl.when(source != slot_me)
         def _():
@@ -368,13 +382,15 @@
     for source in range(1, tps * sps):
         reward = reward + rew_all[source]
     rew_ref[...] = reward
+    for s in range(ranks):
+        order_out[0, s] = order_ref[0, s]
 
     for shift, same in pairs:
         rew_copy(shift, same).wait_send()
     q_copy.wait_send()
 
     def drain(u, carry):
-        hid_copy(u).wait_send()
+        hid_copy(u).wait()
         kv_copy_sibling(u).wait_send()
         for i, step in enumerate(steps):
             @pl.when((dc + step >= 0) & (dc + step < dcs))
@@ -390,6 +406,26 @@
         return carry
 
     lax.fori_loop(0, units, drain, 0)
+
+
+def to_generator_order(ranks, piece, order_ref, hidden, reward_ref, out, out_reward, line, sems):
+    copies = [
+        pltpu.make_async_copy(hidden.at[order_ref[0, s]], out.at[pl.ds(s * piece, piece)], sems.at[s])
+        for s in range(ranks)
+    ]
+    for copy in copies:
+        copy.start()
+    reward = reward_ref[...]
+    segment = lax.broadcasted_iota(jnp.int32, reward.shape, 1) // piece
+    moved = reward
+    for s in range(ranks):
+        shift = lax.rem(s - order_ref[0, s] + ranks, ranks) * piece
+        moved = jnp.where(segment == s, pltpu.roll(reward, shift, 1), moved)
+    line[...] = moved[:1]
+    last = pltpu.make_async_copy(line, out_reward, sems.at[ranks])
+    last.start()
+    for copy in copies + [last]:
+        copy.wait()
 
 
 def gather_body(q_gen, k_gen, value_generator_rows, w_reward, plan, gen_order):
@@ -406,23 +442,30 @@
     units, width = jc * halves, group * HEAD_WIDTH
     sizes = (dcs, sps, tps, piece, rows, heads, group, jc, span, halves)
     bf16, f32 = jnp.bfloat16, jnp.float32
-    vmem, smem = pl.BlockSpec(memory_space=pltpu.VMEM), pl.BlockSpec(memory_space=pltpu.SMEM)
+    vmem, hbm = pl.BlockSpec(memory_space=pltpu.VMEM), pl.BlockSpec(memory_space=pltpu.HBM)
+    smem = pl.BlockSpec(memory_space=pltpu.SMEM)
     dma = pltpu.SemaphoreType.DMA
-    scored, reward = pl.pallas_call(
+    hidden, reward, order = pl.pallas_call(
         functools.partial(gather_attend, sizes),
         out_shape=(
-            jax.ShapeDtypeStruct((ranks, piece, width_q), bf16),
-            jax.ShapeDtypeStruct((8, rows), f32),
+            pltpu.VMEM((ranks, piece, width_q), bf16),
+            pltpu.VMEM((8, rows), f32),
+            pltpu.SMEM(gen_order.shape, jnp.int32),
         ),
-        in_specs=[smem, smem, vmem, vmem, vmem, vmem],
-        out_specs=(vmem, vmem),
+        in_specs=[hbm] * 6,
+        out_specs=(vmem, vmem, smem),
         scratch_shapes=[
+            pltpu.SMEM(gen_order.shape, jnp.int32),
+            pltpu.SMEM(plan.shape, jnp.int32),
+            pltpu.VMEM((ranks, piece, width_q), bf16),
+            pltpu.VMEM((ranks, piece, width_kv), bf16),
+            pltpu.VMEM((ranks, piece, width_kv), bf16),
+            pltpu.VMEM((heads, group, HEAD_WIDTH), f32),
             pltpu.VMEM((units, span, piece, width), bf16),
             pltpu.VMEM((2, units, span, piece, width), bf16),
             pltpu.VMEM((sps, units, 2, span * piece, HEAD_WIDTH), bf16),
             pltpu.VMEM((units, ranks, 2, span * piece, HEAD_WIDTH), bf16),
             pltpu.VMEM((units, span, piece, width), bf16),
-            pltpu.VMEM((sps, units, span, piece, width), bf16),
             pltpu.VMEM((units, 2, span * piece, HEAD_WIDTH), f32),
             pltpu.VMEM((tps * sps + 1, 8, rows), f32),
             dma((units, 4 * sps + 1)),
@@ -434,22 +477,30 @@
             dma((units,)),
             dma((2 * tps,)),
             dma((tps * sps,)),
+            dma((6,)),
         ],
         compiler_params=pltpu.CompilerParams(
             collective_id=0, has_side_effects=True, vmem_limit_bytes=32 * 1024 * 1024
         ),
-    )(
-        gen_order,
-        plan,
-        q_gen.reshape(ranks, piece, width_q),
-        k_gen.reshape(ranks, piece, width_kv),
-        value_generator_rows.reshape(ranks, piece, width_kv),
-        w_reward.reshape(heads, group, HEAD_WIDTH),
-    )
-    labels = jnp.arange(ranks, dtype=jnp.int32)
-    pick = gen_order[0][:, None, None] == labels[None, :, None]
-    reward = jnp.sum(jnp.where(pick, reward[0].reshape(1, ranks, piece), 0.0), axis=1).reshape(rows)
-    return (scored.reshape(rows, width_q), reward)
+    )(*[
+        pltpu.with_memory_space_constraint(operand, pltpu.HBM)
+        for operand in (
+            gen_order,
+            plan,
+            q_gen.reshape(ranks, piece, width_q),
+            k_gen.reshape(ranks, piece, width_kv),
+            value_generator_rows.reshape(ranks, piece, width_kv),
+            w_reward.reshape(heads, group, HEAD_WIDTH),
+        )
+    ])
+    scored, reward = pl.pallas_call(
+        functools.partial(to_generator_order, ranks, piece),
+        out_shape=(pltpu.HBM((rows, width_q), bf16), pltpu.HBM((1, rows), f32)),
+        in_specs=[smem, vmem, vmem],
+        out_specs=(hbm, hbm),
+        scratch_shapes=[pltpu.VMEM((1, rows), f32), dma((ranks + 1,))],
+    )(order, pltpu.with_memory_space_constraint(hidden, pltpu.VMEM), pltpu.with_memory_space_constraint(reward, pltpu.VMEM))
+    return (scored, reward.reshape(rows))
 
 
 def solution(mesh):

time: 38 us -> 32.2 us (0.85)
  local copies, waits for them, and re-layouts: 6.08 us -> 0 us
  Pallas kernels: 30.8 us -> 31.4 us
    unnamed x13 -> x0, local copies, waits for them, and re-layouts: 5.39 us -> none
    reshape x1 -> x0, local copies, waits for them, and re-layouts: 0.59 us -> none  [gather_body(): jnp.sum(jnp.where(pick, reward[0].reshape(1, ranks, piece), 0.0), axis=1)]
    pallas_call x1 -> x2, Pallas kernels: 30.8 us -> 31.4 us  [the longest x1 30.3 us: gather_body(): pl.pallas_call(functools.partial(gather_attend, sizes), out_shape=(pltpu....]
where the time goes in v2:
time: 32.2 us; the launch traced here: 32 us
  Pallas kernels  31.4 us (98%)
  between operations  0.64 us (2%)
    pallas_call x1, Pallas kernels, gather_body(): pl.pallas_call(functools.partial(gather_attend, sizes), out_shape=(pltpu....  30.3 us
    pallas_call x1, Pallas kernels, gather_body(): pl.pallas_call(functools.partial(to_generator_order, ranks, piece), out_s...  1.06 us

profile of v2, /device:TPU:0, one launch (start us, length us, event | category | flops | bytes accessed | tf_op | source)
XLA Modules:
  0.0 32.0 jit_solution(11540814189182580200)
XLA Ops:
  0.6 30.3 %shard_map.77 = (bf16[8,16,4096]{2,1,0:T(8,128)(2,1)S(1)}, f32[8,128]{1,0:T(8,128)S(1)}, s32[1,8]{1,0:T(1,128)S(4)}) custom-call(s32[1,8]{1,0:T(1,128)} %order_hbm.1, s32[3,4]{1,0:T(4,128)} %plan_hbm.1, bf16[8,16,4096]{2,1,0:T(8,128)(2,1)} %bitcast.5, bf16[8,16,512]{2,1,0:T(8,128)(2,1)} %bitcast.6, bf16[8,16,512]{2,1,0:T(8,128)(2,1)} %bitcast.7, ...), custom_call_target="tpu_custom_call" | custom-call | tf_op jit(solution)/shard_map/pallas_call | solution.py:448
  31.0 1.1 %shard_map.78 = (bf16[128,4096]{1,0:T(8,128)(2,1)}, f32[1,128]{1,0:T(1,128)}) custom-call(s32[1,8]{1,0:T(1,128)S(4)} %get-tuple-element.7.order_ref, bf16[8,16,4096]{2,1,0:T(8,128)(2,1)S(1)} %get-tuple-element.8.hidden, f32[8,128]{1,0:T(8,128)S(1)} %get-tuple-element.9.reward_ref), custom_call_target="tpu_custom_call" | custom-call | tf_op jit(solution)/shard_map/pallas_call | solution.py:496

commit v3 on v2

--- a/solution.py
+++ b/solution.py
@@ -177,6 +177,13 @@
 
     steps = [sign * hop for hop in (1, 2) if hop < dcs for sign in (1, -1)]
 
+    def direct(step):
+        target = dc + step
+        inside = (target >= 0) & (target < dcs)
+        return inside if abs(step) == 1 else inside & (target > 0) & (target < dcs - 1)
+
+    relays = ((1, (2, 3), 0), (2, (1, 0), 3)) if dcs == 4 else ()
+
     def kv_copy(u, i, core):
         return pltpu.make_async_remote_copy(
             src_ref=kv_send.at[core, u], dst_ref=kv_all.at[u, me],
@@ -191,11 +198,11 @@
             device_id={"sp": other}, device_id_type=MESH,
         )
 
-    def kv_forward(u, core, source_dc, target_dc):
+    def kv_forward(u, k, core, source_dc, target_dc):
         source = source_dc * sps + core
         return pltpu.make_async_remote_copy(
             src_ref=kv_all.at[u, source], dst_ref=kv_all.at[u, source],
-            send_sem=fwd_ssem.at[u, core], recv_sem=kv_rsem.at[u, source],
+            send_sem=fwd_ssem.at[u, k * sps + core], recv_sem=kv_rsem.at[u, source],
             device_id={"dc": target_dc}, device_id_type=MESH,
         )
 
@@ -213,7 +220,7 @@
 
     def send_unit(u, carry):
         for i, step in enumerate(steps):
-            @pl.when((dc + step >= 0) & (dc + step < dcs))
+            @pl.when(direct(step))
             def _():
                 for core in range(sps):
                     kv_copy(u, i, core).start()
@@ -261,18 +268,18 @@
     def attend(u, carry):
         jj, h = u // halves, lax.rem(u, halves)
         head = sp * jc + jj
-        if dcs == 4:
-            for relay, far, end in ((1, 3, 0), (2, 0, 3)):
-                @pl.when(dc == relay)
-                def _():
+        for relay, fars, end in relays:
+            @pl.when(dc == relay)
+            def _():
+                for k, far in enumerate(fars):
                     for core in range(sps):
                         kv_wait(u, far * sps + core)
-                        kv_forward(u, core, far, end).start()
+                        kv_forward(u, k, core, far, end).start()
         for source in range(ranks):
-            sdc = source // sps
             waits = source != me
-            if dcs == 4 and sdc in (0, 3):
-                waits = waits & (dc != (2 if sdc == 0 else 1))
+            for relay, fars, _ in relays:
+                if source // sps in fars:
+                    waits = waits & (dc != relay)
 
             @pl.when(waits)
             def _():
@@ -393,16 +400,16 @@
         hid_copy(u).wait()
         kv_copy_sibling(u).wait_send()
         for i, step in enumerate(steps):
-            @pl.when((dc + step >= 0) & (dc + step < dcs))
+            @pl.when(direct(step))
             def _():
                 for core in range(sps):
                     kv_copy(u, i, core).wait_send()
-        if dcs == 4:
-            for relay, far, end in ((1, 3, 0), (2, 0, 3)):
-                @pl.when(dc == relay)
-                def _():
+        for relay, fars, end in relays:
+            @pl.when(dc == relay)
+            def _():
+                for k, far in enumerate(fars):
                     for core in range(sps):
-                        kv_forward(u, core, far, end).wait_send()
+                        kv_forward(u, k, core, far, end).wait_send()
         return carry
 
     lax.fori_loop(0, units, drain, 0)
@@ -470,7 +477,7 @@
             pltpu.VMEM((tps * sps + 1, 8, rows), f32),
             dma((units, 4 * sps + 1)),
             dma((units, ranks)),
-            dma((units, sps)),
+            dma((units, 2 * sps)),
             dma,
             dma,
             dma((units,)),

time: 32.2 us -> 31 us (0.963)
  Pallas kernels: 31.4 us -> 30.2 us
    pallas_call x1, Pallas kernels: 30.3 us -> 29.1 us  [gather_body(): pl.pallas_call(functools.partial(gather_attend, sizes), out_shape=(pltpu....]
where the time goes in v3:
time: 31 us; the launch traced here: 30.8 us
  Pallas kernels  30.2 us (97%)
  between operations  0.64 us (2%)
    pallas_call x1, Pallas kernels, gather_body(): pl.pallas_call(functools.partial(gather_attend, sizes), out_shape=(pltpu....  29.1 us
    pallas_call x1, Pallas kernels, gather_body(): pl.pallas_call(functools.partial(to_generator_order, ranks, piece), out_s...  1.06 us

profile of v3, /device:TPU:0, one launch (start us, length us, event | category | flops | bytes accessed | tf_op | source)
XLA Modules:
  0.0 30.8 jit_solution(7990633151739787744)
XLA Ops:
  0.6 29.1 %shard_map.77 = (bf16[8,16,4096]{2,1,0:T(8,128)(2,1)S(1)}, f32[8,128]{1,0:T(8,128)S(1)}, s32[1,8]{1,0:T(1,128)S(4)}) custom-call(s32[1,8]{1,0:T(1,128)} %order_hbm.1, s32[3,4]{1,0:T(4,128)} %plan_hbm.1, bf16[8,16,4096]{2,1,0:T(8,128)(2,1)} %bitcast.5, bf16[8,16,512]{2,1,0:T(8,128)(2,1)} %bitcast.6, bf16[8,16,512]{2,1,0:T(8,128)(2,1)} %bitcast.7, ...), custom_call_target="tpu_custom_call" | custom-call | tf_op jit(solution)/shard_map/pallas_call | solution.py:455
  29.8 1.1 %shard_map.78 = (bf16[128,4096]{1,0:T(8,128)(2,1)}, f32[1,128]{1,0:T(1,128)}) custom-call(s32[1,8]{1,0:T(1,128)S(4)} %get-tuple-element.7.order_ref, bf16[8,16,4096]{2,1,0:T(8,128)(2,1)S(1)} %get-tuple-element.8.hidden, f32[8,128]{1,0:T(8,128)S(1)} %get-tuple-element.9.reward_ref), custom_call_target="tpu_custom_call" | custom-call | tf_op jit(solution)/shard_map/pallas_call | solution.py:503

commit v4 on v3

--- a/solution.py
+++ b/solution.py
@@ -184,32 +184,35 @@
 
     relays = ((1, (2, 3), 0), (2, (1, 0), 3)) if dcs == 4 else ()
 
-    def kv_copy(u, i, core):
+    def cut(ref, *index, part):
+        return ref.at[index if part is None else index + (part,)]
+
+    def kv_copy(u, i, core, part):
         return pltpu.make_async_remote_copy(
-            src_ref=kv_send.at[core, u], dst_ref=kv_all.at[u, me],
-            send_sem=kv_ssem.at[u, i * sps + core], recv_sem=kv_rsem.at[u, me],
+            src_ref=cut(kv_send, core, u, part=part), dst_ref=cut(kv_all, u, me, part=part),
+            send_sem=kv_ssem.at[u, part or 0, i * sps + core], recv_sem=kv_rsem.at[u, part or 0, me],
             device_id={"dc": dc + steps[i], "sp": core}, device_id_type=MESH,
         )
 
-    def kv_copy_sibling(u):
+    def kv_copy_sibling(u, part):
         return pltpu.make_async_remote_copy(
-            src_ref=kv_send.at[other, u], dst_ref=kv_all.at[u, me],
-            send_sem=kv_ssem.at[u, len(steps) * sps], recv_sem=kv_rsem.at[u, me],
+            src_ref=cut(kv_send, other, u, part=part), dst_ref=cut(kv_all, u, me, part=part),
+            send_sem=kv_ssem.at[u, part or 0, len(steps) * sps], recv_sem=kv_rsem.at[u, part or 0, me],
             device_id={"sp": other}, device_id_type=MESH,
         )
 
-    def kv_forward(u, k, core, source_dc, target_dc):
+    def kv_forward(u, k, core, source_dc, target_dc, part):
         source = source_dc * sps + core
         return pltpu.make_async_remote_copy(
-            src_ref=kv_all.at[u, source], dst_ref=kv_all.at[u, source],
-            send_sem=fwd_ssem.at[u, k * sps + core], recv_sem=kv_rsem.at[u, source],
+            src_ref=cut(kv_all, u, source, part=part), dst_ref=cut(kv_all, u, source, part=part),
+            send_sem=fwd_ssem.at[u, part or 0, k * sps + core], recv_sem=kv_rsem.at[u, part or 0, source],
             device_id={"dc": target_dc}, device_id_type=MESH,
         )
 
-    def kv_wait(u, source):
+    def kv_wait(u, source, part):
         pltpu.make_async_remote_copy(
-            src_ref=kv_all.at[u, source], dst_ref=kv_all.at[u, source],
-            send_sem=kv_ssem.at[u, 0], recv_sem=kv_rsem.at[u, source],
+            src_ref=cut(kv_all, u, source, part=part), dst_ref=cut(kv_all, u, source, part=part),
+            send_sem=kv_ssem.at[u, part or 0, 0], recv_sem=kv_rsem.at[u, part or 0, source],
             device_id={"sp": other}, device_id_type=MESH,
         ).wait_recv()
 
@@ -218,17 +221,25 @@
         device_id={"sp": other}, device_id_type=MESH,
     )
 
-    def send_unit(u, carry):
+    def send_unit(u, part):
         for i, step in enumerate(steps):
             @pl.when(direct(step))
             def _():
                 for core in range(sps):
-                    kv_copy(u, i, core).start()
-        kv_copy_sibling(u).start()
+                    kv_copy(u, i, core, part).start()
+        kv_copy_sibling(u, part).start()
+
+    last = units - 1
+
+    def send_whole(u, carry):
+        send_unit(u, None)
+        return carry
+
+    lax.fori_loop(0, last, send_whole, 0)
+    for part in range(2):
+        send_unit(last, part)
+    for u in range(units):
         kv_all[u, me] = kv_send[sp, u]
-        return carry
-
-    lax.fori_loop(0, units, send_unit, 0)
     loads[3].wait()
     for d in range(ranks):
         h, dl = d // span, d % span
@@ -263,18 +274,16 @@
             device_id={"sp": other}, device_id_type=MESH,
         )
 
-    q_copy.wait_recv()
-
-    def attend(u, carry):
-        jj, h = u // halves, lax.rem(u, halves)
-        head = sp * jc + jj
+    def pass_on(u, part):
         for relay, fars, end in relays:
             @pl.when(dc == relay)
             def _():
                 for k, far in enumerate(fars):
                     for core in range(sps):
-                        kv_wait(u, far * sps + core)
-                        kv_forward(u, k, core, far, end).start()
+                        kv_wait(u, far * sps + core, part)
+                        kv_forward(u, k, core, far, end, part).start()
+
+    def arrive(u, part):
         for source in range(ranks):
             waits = source != me
             for relay, fars, _ in relays:
@@ -283,7 +292,11 @@
 
             @pl.when(waits)
             def _():
-                kv_wait(u, source)
+                kv_wait(u, source, part)
+
+    def attend(u, split):
+        jj, h = u // halves, lax.rem(u, halves)
+        head = sp * jc + jj
 
         def plan_order(which):
             return jnp.concatenate(
@@ -295,7 +308,9 @@
                 axis=0,
             )
 
-        keys, values = plan_order(0), plan_order(1)
+        arrive(u, 0 if split else None)
+        keys = plan_order(0)
+        weighed = []
         for dl in range(span):
             d = h * span + dl
             slot = d // sps
@@ -330,9 +345,15 @@
                 total = total + weight
             total = jnp.sum(total, axis=1, keepdims=True)
             weight16 = jnp.concatenate([weight.astype(jnp.bfloat16) for weight in weights], axis=1)
-            mixed = jnp.dot(weight16, values[:n], preferred_element_type=jnp.float32)
             base = (slot - start) * (rows * sps) + lax.rem(d, sps) * rows
             share = jnp.where(offset + base < plan_ref[2, slot], 1.0 / total, 0.0)
+            weighed.append((weight16, share))
+        if split:
+            arrive(u, 1)
+        values = plan_order(1)
+        for dl, (weight16, share) in enumerate(weighed):
+            d = h * span + dl
+            mixed = jnp.dot(weight16, values[:(dl + 1) * rows], preferred_element_type=jnp.float32)
             hidden = (mixed * share).astype(jnp.bfloat16)
             for t in range(2):
                 reward = jnp.zeros((piece, HEAD_WIDTH), jnp.float32)
@@ -347,9 +368,21 @@
                     reward = reward + part.astype(jnp.float32) * w
                 racc[u, t, pl.ds(dl * piece, piece), :] = reward
         hid_copy(u).start()
+
+    def attend_whole(u, carry):
+        attend(u, False)
         return carry
 
-    lax.fori_loop(0, units, attend, 0)
+    def pass_on_whole(u, carry):
+        pass_on(u, None)
+        return carry
+
+    lax.fori_loop(0, last, pass_on_whole, 0)
+    for part in range(2):
+        pass_on(last, part)
+    q_copy.wait_recv()
+    lax.fori_loop(0, last, attend_whole, 0)
+    attend(jnp.int32(last), True)
 
     sums = []
     for t in range(2):
@@ -373,9 +406,37 @@
             device_id={"tp": peer, "sp": sp if same else other}, device_id_type=MESH,
         )
 
-    pairs = [(shift, same) for shift in range(tps) for same in (True, False) if (shift, same) != (0, True)]
+    pairs = [(shift, same) for shift in reversed(range(tps)) for same in (True, False) if (shift, same) != (0, True)]
     for shift, same in pairs:
         rew_copy(shift, same).start()
+
+    for shift, same in pairs:
+        rew_copy(shift, same).wait_send()
+    q_copy.wait_send()
+
+    def drain(u, part):
+        kv_copy_sibling(u, part).wait_send()
+        for i, step in enumerate(steps):
+            @pl.when(direct(step))
+            def _():
+                for core in range(sps):
+                    kv_copy(u, i, core, part).wait_send()
+        for relay, fars, end in relays:
+            @pl.when(dc == relay)
+            def _():
+                for k, far in enumerate(fars):
+                    for core in range(sps):
+                        kv_forward(u, k, core, far, end, part).wait_send()
+
+    def drain_whole(u, carry):
+        drain(u, None)
+        return carry
+
+    lax.fori_loop(0, last, drain_whole, 0)
+    for part in range(2):
+        drain(last, part)
+    for u in range(units):
+        hid_copy(u).wait()
 
     for source in range(tps * sps):
         @pl.when(source != slot_me)
@@ -391,28 +452,6 @@
     rew_ref[...] = reward
     for s in range(ranks):
         order_out[0, s] = order_ref[0, s]
-
-    for shift, same in pairs:
-        rew_copy(shift, same).wait_send()
-    q_copy.wait_send()
-
-    def drain(u, carry):
-        hid_copy(u).wait()
-        kv_copy_sibling(u).wait_send()
-        for i, step in enumerate(steps):
-            @pl.when(direct(step))
-            def _():
-                for core in range(sps):
-                    kv_copy(u, i, core).wait_send()
-        for relay, fars, end in relays:
-            @pl.when(dc == relay)
-            def _():
-                for k, far in enumerate(fars):
-                    for core in range(sps):
-                        kv_forward(u, k, core, far, end).wait_send()
-        return carry
-
-    lax.fori_loop(0, units, drain, 0)
 
 
 def to_generator_order(ranks, piece, order_ref, hidden, reward_ref, out, out_reward, line, sems):
@@ -475,9 +514,9 @@
             pltpu.VMEM((units, span, piece, width), bf16),
             pltpu.VMEM((units, 2, span * piece, HEAD_WIDTH), f32),
             pltpu.VMEM((tps * sps + 1, 8, rows), f32),
-            dma((units, 4 * sps + 1)),
-            dma((units, ranks)),
-            dma((units, 2 * sps)),
+            dma((units, 2, 4 * sps + 1)),
+            dma((units, 2, ranks)),
+            dma((units, 2, 2 * sps)),
             dma,
             dma,
             dma((units,)),

time: 31 us -> 30.6 us (0.987)
  Pallas kernels: 30.2 us -> 29.8 us
    pallas_call x1, Pallas kernels: 29.1 us -> 28.8 us  [gather_body(): pl.pallas_call(functools.partial(gather_attend, sizes), out_shape=(pltpu....]
where the time goes in v4:
time: 30.6 us; the launch traced here: 30.5 us
  Pallas kernels  29.8 us (97%)
  between operations  0.64 us (2%)
    pallas_call x1, Pallas kernels, gather_body(): pl.pallas_call(functools.partial(gather_attend, sizes), out_shape=(pltpu....  28.8 us
    pallas_call x1, Pallas kernels, gather_body(): pl.pallas_call(functools.partial(to_generator_order, ranks, piece), out_s...  1.06 us

profile of v4, /device:TPU:0, one launch (start us, length us, event | category | flops | bytes accessed | tf_op | source)
XLA Modules:
  0.0 30.5 jit_solution(11727617272521010684)
XLA Ops:
  0.6 28.8 %shard_map.77 = (bf16[8,16,4096]{2,1,0:T(8,128)(2,1)S(1)}, f32[8,128]{1,0:T(8,128)S(1)}, s32[1,8]{1,0:T(1,128)S(4)}) custom-call(s32[1,8]{1,0:T(1,128)} %order_hbm.1, s32[3,4]{1,0:T(4,128)} %plan_hbm.1, bf16[8,16,4096]{2,1,0:T(8,128)(2,1)} %bitcast.5, bf16[8,16,512]{2,1,0:T(8,128)(2,1)} %bitcast.6, bf16[8,16,512]{2,1,0:T(8,128)(2,1)} %bitcast.7, ...), custom_call_target="tpu_custom_call" | custom-call | tf_op jit(solution)/shard_map/pallas_call | solution.py:494
  29.4 1.1 %shard_map.78 = (bf16[128,4096]{1,0:T(8,128)(2,1)}, f32[1,128]{1,0:T(1,128)}) custom-call(s32[1,8]{1,0:T(1,128)S(4)} %get-tuple-element.7.order_ref, bf16[8,16,4096]{2,1,0:T(8,128)(2,1)S(1)} %get-tuple-element.8.hidden, f32[8,128]{1,0:T(8,128)S(1)} %get-tuple-element.9.reward_ref), custom_call_target="tpu_custom_call" | custom-call | tf_op jit(solution)/shard_map/pallas_call | solution.py:542

commit v5 on v4

--- a/solution.py
+++ b/solution.py
@@ -140,7 +140,7 @@
 
     arguments = ((order_hbm, order_ref), (k_hbm, k_ref), (v_hbm, v_ref), (q_hbm, q_ref), (plan_hbm, plan_ref), (w_hbm, w_ref))
     loads = [pltpu.make_async_copy(a, b, in_sem.at[i]) for i, (a, b) in enumerate(arguments)]
-    for load in loads:
+    for load in loads[:3]:
         load.start()
 
     barrier = pltpu.get_barrier_semaphore()
@@ -158,21 +158,24 @@
 
     for load in loads[:3]:
         load.wait()
+    for load in loads[3:]:
+        load.start()
     segments = []
     for d in range(ranks):
         seg = jnp.int32(0)
         for s in range(1, ranks):
             seg = jnp.where(order_ref[0, s] == d, s, seg)
         segments.append(seg)
-    for d in range(ranks):
-        h, dl = d // span, d % span
-        for jj in range(jc):
-            u = jj * halves + h
+    def prepare(u):
+        jj, h = u // halves, u % halves
+        for dl in range(span):
+            seg = segments[h * span + dl]
             for core in range(sps):
                 cols = pl.ds((core * jc + jj) * HEAD_WIDTH, HEAD_WIDTH)
-                kv_send[core, u, 0, pl.ds(dl * piece, piece), :] = k_ref[segments[d], :, cols]
-                kv_send[core, u, 1, pl.ds(dl * piece, piece), :] = v_ref[segments[d], :, cols]
-
+                kv_send[core, u, 0, pl.ds(dl * piece, piece), :] = k_ref[seg, :, cols]
+                kv_send[core, u, 1, pl.ds(dl * piece, piece), :] = v_ref[seg, :, cols]
+
+    prepare(0)
     pl.semaphore_wait(barrier, ranks - 1 + (tps - 1) * sps)
 
     steps = [sign * hop for hop in (1, 2) if hop < dcs for sign in (1, -1)]
@@ -231,11 +234,9 @@
 
     last = units - 1
 
-    def send_whole(u, carry):
+    for u in range(last):
         send_unit(u, None)
-        return carry
-
-    lax.fori_loop(0, last, send_whole, 0)
+        prepare(u + 1)
     for part in range(2):
         send_unit(last, part)
     for u in range(units):
@@ -384,7 +385,18 @@
     lax.fori_loop(0, last, attend_whole, 0)
     attend(jnp.int32(last), True)
 
-    sums = []
+    slot_me = tp * sps + sp
+
+    def rew_copy(shift, same):
+        peer = lax.rem(tp + shift, tps)
+        return pltpu.make_async_remote_copy(
+            src_ref=rew_all.at[slot_me if same else tps * sps], dst_ref=rew_all.at[slot_me],
+            send_sem=rew_ssem.at[2 * shift + (0 if same else 1)], recv_sem=rew_rsem.at[slot_me],
+            device_id={"tp": peer, "sp": sp if same else other}, device_id_type=MESH,
+        )
+
+    pairs = [(shift, same) for shift in reversed(range(tps)) for same in (True, False) if (shift, same) != (0, True)]
+
     for t in range(2):
         cells = []
         for h in range(halves):
@@ -393,22 +405,10 @@
                 cell = cell + racc[jj * halves + h, t]
             cells.append(cell)
         line = jnp.sum(jnp.concatenate(cells, axis=0).T, axis=0, keepdims=True)
-        sums.append(jnp.broadcast_to(line, (8, rows)))
-    slot_me = tp * sps + sp
-    rew_all[tps * sps] = sums[1]
-    rew_all[slot_me] = sums[0]
-
-    def rew_copy(shift, same):
-        peer = lax.rem(tp + shift, tps)
-        return pltpu.make_async_remote_copy(
-            src_ref=rew_all.at[slot_me if same else tps * sps], dst_ref=rew_all.at[slot_me],
-            send_sem=rew_ssem.at[2 * shift + (0 if same else 1)], recv_sem=rew_rsem.at[slot_me],
-            device_id={"tp": peer, "sp": sp if same else other}, device_id_type=MESH,
-        )
-
-    pairs = [(shift, same) for shift in reversed(range(tps)) for same in (True, False) if (shift, same) != (0, True)]
-    for shift, same in pairs:
-        rew_copy(shift, same).start()
+        rew_all[slot_me if t == 0 else tps * sps] = jnp.broadcast_to(line, (8, rows))
+        for shift, same in pairs:
+            if same == (t == 0):
+                rew_copy(shift, same).start()
 
     for shift, same in pairs:
         rew_copy(shift, same).wait_send()

time: 30.6 us -> 30.6 us (level)
  no operation moved by 1% of the time
where the time goes in v5:
time: 30.6 us; the launch traced here: 30.5 us
  Pallas kernels  29.8 us (97%)
  between operations  0.64 us (2%)
    pallas_call x1, Pallas kernels, gather_body(): pl.pallas_call(functools.partial(gather_attend, sizes), out_shape=(pltpu....  28.8 us
    pallas_call x1, Pallas kernels, gather_body(): pl.pallas_call(functools.partial(to_generator_order, ranks, piece), out_s...  1.06 us

profile of v5, /device:TPU:0, one launch (start us, length us, event | category | flops | bytes accessed | tf_op | source)
XLA Modules:
  0.0 30.5 jit_solution(8930656071332661258)
XLA Ops:
  0.6 28.8 %shard_map.77 = (bf16[8,16,4096]{2,1,0:T(8,128)(2,1)S(1)}, f32[8,128]{1,0:T(8,128)S(1)}, s32[1,8]{1,0:T(1,128)S(4)}) custom-call(s32[1,8]{1,0:T(1,128)} %order_hbm.1, s32[3,4]{1,0:T(4,128)} %plan_hbm.1, bf16[8,16,4096]{2,1,0:T(8,128)(2,1)} %bitcast.5, bf16[8,16,512]{2,1,0:T(8,128)(2,1)} %bitcast.6, bf16[8,16,512]{2,1,0:T(8,128)(2,1)} %bitcast.7, ...), custom_call_target="tpu_custom_call" | custom-call | tf_op jit(solution)/shard_map/pallas_call | solution.py:494
  29.4 1.1 %shard_map.78 = (bf16[128,4096]{1,0:T(8,128)(2,1)}, f32[1,128]{1,0:T(1,128)}) custom-call(s32[1,8]{1,0:T(1,128)S(4)} %get-tuple-element.7.order_ref, bf16[8,16,4096]{2,1,0:T(8,128)(2,1)S(1)} %get-tuple-element.8.hidden, f32[8,128]{1,0:T(8,128)S(1)} %get-tuple-element.9.reward_ref), custom_call_target="tpu_custom_call" | custom-call | tf_op jit(solution)/shard_map/pallas_call | solution.py:542
